TPU v7x, 32 devices: a whole 2x2x4 slice. The times are simulated.
32 devices in a mesh: group: 2 (over y), expert: 16 (over z, x, core).
Axes of the slice: x: 2, y: 2, z: 4, core: 2. Of those that a mesh axis runs over, the one named last changes fastest.
Arguments:
- tokens: bfloat16 [2048, 3072], P(('group', 'expert')), parts along dimension 0, may hold values from -6 to 6
- expert_ids: int32 [2048, 4], P(('group', 'expert')), parts along dimension 0, may hold values from 0 to 15, all different within a row; in each aligned block of 64 rows (0 to 63, 64 to 127, ...) at most 18 rows name the same one
- gate_fixed: int32 [2048, 4], P(('group', 'expert')), parts along dimension 0, may hold values from 1 to 65535
- gate_q: bfloat16 [3072, 43008], P(None, 'expert'), may hold values from -127 to 127
- up_q: bfloat16 [3072, 43008], P(None, 'expert'), may hold values from -127 to 127
- down_q: bfloat16 [43008, 3072], P('expert'), may hold values from -127 to 127
- gate_scale: float32 [43008], P('expert'), as said below
- up_scale: float32 [43008], P('expert'), as said below
- down_scale: float32 [8, 3072], replicated, as said below
Outputs:
- mixed: bfloat16 [2048, 3072], P(('group', 'expert')), parts along dimension 0
There are 2 independent parts, one for each index of `group`. A program takes and returns all parts, laid end to end along the dimension named above; an argument that names none is the same for every part. Nothing has to cross between parts.
Inputs may be any that keep to these rules, and one draw needn't show every extreme that they name: `expert_ids`: each row names 4 different experts; among the 64 rows of one device at most 18 name one expert, and some device reaches 18. `gate_scale`: Positive. `up_scale`: Positive. `down_scale`: Positive.
All inputs are finite; a program needn't handle non-finite values.
Results may differ from a plain program's by a relative error of at most 0.0085.
Values may be sent and summed in bfloat16 or wider, within the bound.
A program may use at most 128 MiB of HBM per device.

v0:
```python
import jax
import jax.numpy as jnp
from jax import lax
from jax.sharding import PartitionSpec as P

EXPERTS = 16
WINDOW = 8
CAP = 18


def expert_block(routed_rows, gate_q, up_q, down_q, gate_scale, up_scale, scale_row):
    gate_out = (
        jnp.dot(routed_rows, gate_q, preferred_element_type=jnp.float32) * gate_scale[None, :]
    )
    up_out = jnp.dot(routed_rows, up_q, preferred_element_type=jnp.float32) * up_scale[None, :]
    hidden = (jax.nn.silu(gate_out) * up_out).astype(jnp.bfloat16)
    partial_value = jnp.dot(hidden, down_q, preferred_element_type=jnp.float32) * scale_row
    return partial_value.astype(jnp.bfloat16)


def shards(tokens, expert_ids, gate_fixed, gate_q, up_q, down_q, gate_scale, up_scale, down_scale):
    devices = lax.axis_size("expert")
    splits = devices // WINDOW
    expert = lax.axis_index("expert") // splits
    width = tokens.shape[1]
    scale_row = lax.dynamic_slice_in_dim(down_scale, expert, 1, 0)
    experts_all = jnp.arange(EXPERTS, dtype=jnp.int32)
    slot_ids = jnp.arange(CAP, dtype=jnp.int32)
    onehot = expert_ids[:, :, None] == experts_all[None, None, :]
    chosen = jnp.any(onehot, axis=1).astype(jnp.int32)[:, :WINDOW]
    rank_in = jnp.cumsum(chosen, axis=0) - chosen
    placing = (chosen.T[:, None, :] == 1) & (rank_in.T[:, None, :] == slot_ids[None, :, None])
    outgoing = jnp.einsum(
        "ect,td->ecd", placing.astype(jnp.bfloat16), tokens, preferred_element_type=jnp.float32
    ).astype(jnp.bfloat16)
    outgoing = jnp.broadcast_to(outgoing[:, None], (WINDOW, splits, CAP, width)).reshape(
        devices, CAP, width
    )
    received = lax.all_to_all(outgoing, "expert", split_axis=0, concat_axis=0, tiled=True)
    slot_count = received.shape[1]
    flat_rows = received.reshape(devices * slot_count, width)
    partial_value = expert_block(flat_rows, gate_q, up_q, down_q, gate_scale, up_scale, scale_row)
    returned = lax.all_to_all(
        partial_value.reshape(devices, slot_count, width),
        "expert",
        split_axis=0,
        concat_axis=0,
        tiled=True,
    )
    expert_out = jnp.sum(returned.astype(jnp.float32).reshape(WINDOW, splits, CAP, width), axis=1)
    fixed = gate_fixed.astype(jnp.float32)
    weight = fixed / jnp.sum(fixed, axis=1, keepdims=True)
    token_weight = jnp.sum(onehot.astype(jnp.float32) * weight[:, :, None], axis=1)[:, :WINDOW]
    combining = placing.astype(jnp.float32) * token_weight.T[:, None, :]
    mixed = jnp.einsum("ect,ecd->td", combining, expert_out, precision=lax.Precision.HIGHEST)
    return mixed.astype(jnp.bfloat16)


def solution(mesh):
    placed = (
        P(("group", "expert"), None),
        P(("group", "expert"), None),
        P(("group", "expert"), None),
        P(None, "expert"),
        P(None, "expert"),
        P("expert", None),
        P("expert"),
        P("expert"),
        P(),
    )
    return jax.shard_map(
        shards, mesh=mesh, in_specs=placed, out_specs=P(("group", "expert"), None), check_vma=False
    )
```

profile of v0, /device:TPU:11, one launch (start us, length us, event | category | flops | bytes accessed | tf_op | source)
XLA Modules:
  0.0 164.6 jit_solution(4334525957954813695)
XLA Ops:
  0.0 0.0 copy-start
  0.0 0.7 fusion.17
  0.8 0.1 copy.18
  0.9 0.1 reduce_window_sum.11
  1.0 0.1 copy.20
  1.0 0.1 copy.19
  1.1 0.0 copy-done
  1.1 0.5 convolution_convert_fusion
  1.6 1.7 %broadcast_in_dim.2 = bf16[8,2,18,3072]{3,2,1,0:T(8,128)(2,1)} broadcast(bf16[8,18,3072]{2,1,0:T(8,128)(2,1)S(1)} %convolution_convert_fusion), dimensions={0,2,3} | broadcast | bytes 2654208 | tf_op jit(solution)/shard_map/broadcast_in_dim | solution.py:36
  3.3 6.6 %all-to-all-start = ((bf16[16,18,3072]{2,1,0:T(8,128)(2,1)}), bf16[16,18,3072]{2,1,0:T(8,128)(2,1)S(1)}, u32[]{:S(2)}, u32[]{:S(2)}) async-start(bf16[16,18,3072]{2,1,0:T(8,128)(2,1)} %bitcast.24), calls=%async_computation | async-start | bytes 4718592 | tf_op jit(solution)/shard_map/all_to_all | solution.py:39
  9.9 0.0 copy-start.5
  9.9 0.9 constant_dynamic-slice_fusion
  10.8 52.1 %all-to-all-done = bf16[16,18,3072]{2,1,0:T(8,128)(2,1)S(1)} async-done(((bf16[16,18,3072]{2,1,0:T(8,128)(2,1)}), bf16[16,18,3072]{2,1,0:T(8,128)(2,1)S(1)}, u32[]{:S(2)}, u32[]{:S(2)}) %all-to-all-start) | async-done | bytes 1769504 | tf_op jit(solution)/shard_map/all_to_all | solution.py:39
  62.9 1.5 reshape.26
  64.4 0.0 copy-done.5
  64.4 0.0 copy-start.2
  64.4 0.0 copy-start.6
  64.4 12.6 %convolution_multiply_fusion.1 = f32[288,2688]{1,0:T(8,128)} fusion(bf16[288,3072]{1,0:T(8,128)(2,1)} %reshape.26, bf16[3072,2688]{1,0:T(8,128)(2,1)} %param.12, f32[2688]{0:T(1024)S(1)} %copy-done.5), kind=kOutput, calls=%fused_computation.3 | convolution fusion | flops 4757114880 | bytes 21391872 | tf_op jit(solution)/shard_map/dot_general | solution.py:13
  77.1 0.0 copy-done.2
  77.1 0.0 copy-done.6
  77.1 23.8 %fusion.1 = bf16[288,3072]{1,0:T(8,128)(2,1)} fusion(bf16[2688,3072]{1,0:T(8,128)(2,1)} %param.14, bf16[288,3072]{1,0:T(8,128)(2,1)S(1)} %copy-done.2, bf16[3072,2688]{1,0:T(8,128)(2,1)} %param.13, f32[288,2688]{1,0:T(8,128)} %convolution_multiply_fusion.1, f32[3072]{0:T(1024)S(1)} %bitcast.25, f32[2688]{0:T(1024)S(1)} %copy-done.6), kind=kOutput, calls=%fused_computation.5 | convolution fusion | flops 9519869952 | bytes 39688704 | tf_op jit(solution)/shard_map/dot_general | solution.py:17
  100.8 2.8 %reshape.27 = bf16[16,18,3072]{2,1,0:T(8,128)(2,1)} reshape(bf16[288,3072]{1,0:T(8,128)(2,1)} %fusion.1) | data formatting | bytes 3538944 | tf_op jit(solution)/shard_map/reshape | solution.py:44
  103.7 0.0 copy-start.3
  103.7 0.0 copy-start.4
  103.7 5.1 %all-to-all-start.1 = ((bf16[16,18,3072]{2,1,0:T(8,128)(2,1)}), bf16[16,18,3072]{2,1,0:T(8,128)(2,1)S(1)}, u32[]{:S(2)}, u32[]{:S(2)}) async-start(bf16[16,18,3072]{2,1,0:T(8,128)(2,1)} %reshape.27), calls=%async_computation.1 | async-start | bytes 4718592 | tf_op jit(solution)/shard_map/all_to_all | solution.py:43
  108.7 0.0 copy-done.3
  108.8 0.0 copy-done.4
  108.8 0.0 copy-start.1
  108.8 52.9 %all-to-all-done.1 = bf16[16,18,3072]{2,1,0:T(8,128)(2,1)S(1)} async-done(((bf16[16,18,3072]{2,1,0:T(8,128)(2,1)}), bf16[16,18,3072]{2,1,0:T(8,128)(2,1)S(1)}, u32[]{:S(2)}, u32[]{:S(2)}) %all-to-all-start.1) | async-done | bytes 1769504 | tf_op jit(solution)/shard_map/all_to_all | solution.py:43
  161.8 0.5 convert_reduce_fusion
  162.3 2.4 %fusion.3 = bf16[64,3072]{1,0:T(8,128)(2,1)} fusion(f32[8,18,3072]{2,1,0:T(8,128)S(1)} %convert_reduce_fusion, f32[8,64]{1,0:T(8,128)S(1)} %slice_bitcast_fusion, s32[8,64]{1,0:T(8,128)S(1)} %copy.20, pred[8,64]{1,0:T(8,128)(4,1)S(1)} %copy.19), kind=kOutput, calls=%fused_computation.9 | convolution fusion | flops 339962880 | bytes 2167296 | tf_op jit(solution)/shard_map/ect,ecd->td/dot_general | solution.py:55
  164.6 0.0 copy-done.1
  (7 shorter events, 0.1 us)
Async XLA Ops:
  0.0 1.1 copy-start
  3.3 59.6 %all-to-all-start = ((bf16[16,18,3072]{2,1,0:T(8,128)(2,1)}), bf16[16,18,3072]{2,1,0:T(8,128)(2,1)S(1)}, u32[]{:S(2)}, u32[]{:S(2)}) async-start(bf16[16,18,3072]{2,1,0:T(8,128)(2,1)} %bitcast.24), calls=%async_computation | async-start | bytes 4718592 | tf_op jit(solution)/shard_map/all_to_all | solution.py:39
  9.9 54.6 %copy-start.5 = (f32[2688]{0:T(1024)S(1)}, f32[2688]{0:T(1024)}, u32[]{:S(2)}) copy-start(f32[2688]{0:T(1024)} %param.15) | copy-start | bytes 32260
  64.4 12.6 %copy-start.2 = (bf16[288,3072]{1,0:T(8,128)(2,1)S(1)}, bf16[288,3072]{1,0:T(8,128)(2,1)}, u32[]{:S(2)}) copy-start(bf16[288,3072]{1,0:T(8,128)(2,1)} %reshape.26) | copy-start | bytes 5308420
  64.4 12.6 %copy-start.6 = (f32[2688]{0:T(1024)S(1)}, f32[2688]{0:T(1024)}, u32[]{:S(2)}) copy-start(f32[2688]{0:T(1024)} %param.16) | copy-start | bytes 32260
  103.7 5.1 %copy-start.3 = (s32[64,4]{0,1:T(4,128)S(1)}, s32[64,4]{0,1:T(4,128)}, u32[]{:S(2)}) copy-start(s32[64,4]{0,1:T(4,128)} %param.11) | copy-start | bytes 3076
  103.7 5.1 %copy-start.4 = (s32[64,4]{0,1:T(4,128)S(1)}, s32[64,4]{0,1:T(4,128)}, u32[]{:S(2)}) copy-start(s32[64,4]{0,1:T(4,128)} %param.10) | copy-start | bytes 3076
  103.7 58.1 %all-to-all-start.1 = ((bf16[16,18,3072]{2,1,0:T(8,128)(2,1)}), bf16[16,18,3072]{2,1,0:T(8,128)(2,1)S(1)}, u32[]{:S(2)}, u32[]{:S(2)}) async-start(bf16[16,18,3072]{2,1,0:T(8,128)(2,1)} %reshape.27), calls=%async_computation.1 | async-start | bytes 4718592 | tf_op jit(solution)/shard_map/all_to_all | solution.py:43
  108.8 55.9 %copy-start.1 = (bf16[64,3072]{1,0:T(8,128)(2,1)S(1)}, bf16[64,3072]{1,0:T(8,128)(2,1)}, u32[]{:S(2)}) copy-start(bf16[64,3072]{1,0:T(8,128)(2,1)} %param.9) | copy-start | bytes 1179652
where the time goes:
time: 165 us
  waiting for transfers between devices  105 us (64%)
  matrix products  39.2 us (24%)
  starting transfers between devices  11.6 us (7%)
  local copies, waits for them, and re-layouts  7.26 us (4%)
    all_to_all x1, waiting for transfers between devices, shards(): lax.all_to_all(partial_value.reshape(devices, slot_count, width), 'expert...  52.9 us
    all_to_all x1, waiting for transfers between devices, shards(): lax.all_to_all(outgoing, 'expert', split_axis=0, concat_axis=0, tiled=True)  52.1 us
    dot_general x1, matrix products, expert_block(): jnp.dot(hidden, down_q, preferred_element_type=jnp.float32) * scale_row  23.8 us
    dot_general x1, matrix products, expert_block(): jnp.dot(routed_rows, gate_q, preferred_element_type=jnp.float32)  12.6 us
    all_to_all x1, starting transfers between devices, shards(): lax.all_to_all(outgoing, 'expert', split_axis=0, concat_axis=0, tiled=True)  6.55 us
    all_to_all x1, starting transfers between devices, shards(): lax.all_to_all(partial_value.reshape(devices, slot_count, width), 'expert...  5.05 us
  transfers between devices with their start and end apart: 2, of which 2 were waited for; matrix products, arithmetic and copies ran while one was open for 1% of the time, Pallas kernels for 0%

commit v1 on v0

--- a/solution.py
+++ b/solution.py
@@ -1,6 +1,10 @@
+import functools
+
 import jax
 import jax.numpy as jnp
 from jax import lax
+from jax.experimental import pallas as pl
+from jax.experimental.pallas import tpu as pltpu
 from jax.sharding import PartitionSpec as P
 
 EXPERTS = 16
@@ -56,6 +60,311 @@
     return mixed.astype(jnp.bfloat16)
 
 
+MESH = pl.DeviceIdType.MESH
+BASE = 16
+OVER = CAP - BASE
+CHIPS = WINDOW
+ROWS = CHIPS * BASE
+HALF = ROWS + CHIPS * OVER
+LANES = 128
+PIECES = BASE // OVER
+CHUNK = PIECES * LANES
+WIDE = CHUNK + LANES
+TILE = 512
+
+
+def iota(shape, dim):
+    return lax.broadcasted_iota(jnp.int32, shape, dim)
+
+
+def fused_kernel(
+    tokens, ids, fixed, gate_w, up_w, down_w, gate_scale, up_scale, down_scale, out,
+    wg, wu, wd, recv, send, back, acc_g, acc_u, hidden, sib,
+    w_sem, d_sem, send_sem, recv_sem, fwd_send, fwd_recv, sib_send, sib_recv, back_send, back_recv,
+):
+    me = lax.axis_index("expert")
+    chip = me // 2
+    core = me % 2
+    sibling = chip * 2 + 1 - core
+    chunks = tokens.shape[1] // CHUNK
+    units = wg.shape[2]
+    toks = tokens.shape[0]
+
+    def weight_copy(c, which):
+        w, buf = ((gate_w, wg), (up_w, wu))[which]
+        return pltpu.make_async_copy(w.at[pl.ds(c * CHUNK, CHUNK), :], buf.at[c], w_sem.at[c, which])
+
+    def down_copy(d):
+        return pltpu.make_async_copy(
+            down_w.at[:, pl.ds(d * CHUNK, CHUNK)], wd.at[d % 2], d_sem.at[d % 2]
+        )
+
+    def peer(p):
+        return ((chip + p) % CHIPS) * 2 + core
+
+    mine = pl.multiple_of(core * HALF, 16)
+    other = pl.multiple_of((1 - core) * HALF, 16)
+    slot = pl.multiple_of(chip * BASE, 16)
+
+    barrier = pltpu.get_barrier_semaphore()
+    pl.semaphore_signal(barrier, inc=1, device_id={"expert": sibling}, device_id_type=MESH)
+    for p in range(1, CHIPS):
+        pl.semaphore_signal(barrier, inc=1, device_id={"expert": peer(p)}, device_id_type=MESH)
+
+    for c in range(chunks):
+        weight_copy(c, 0).start()
+        weight_copy(c, 1).start()
+    for d in range(2):
+        down_copy(d).start()
+
+    lane = iota((toks, LANES), 1)
+    chosen = jnp.zeros((toks, LANES), jnp.float32)
+    weight = jnp.zeros((toks, LANES), jnp.float32)
+    fx = fixed[...].astype(jnp.float32)
+    total = jnp.sum(fx, axis=1, keepdims=True)
+    idv = ids[...]
+    for k in range(idv.shape[1]):
+        hit = (idv[:, k : k + 1] == lane // BASE).astype(jnp.float32)
+        chosen = chosen + hit
+        weight = weight + hit * (fx[:, k : k + 1] / total)
+    before = (iota((toks, toks), 0) > iota((toks, toks), 1)).astype(jnp.bfloat16)
+    rank = jnp.dot(before, chosen.astype(jnp.bfloat16), preferred_element_type=jnp.float32)
+    main_t = jnp.where(rank == (lane % BASE).astype(jnp.float32), chosen, 0.0)
+    over_t = jnp.where(rank == (BASE + lane % OVER).astype(jnp.float32), chosen, 0.0)
+    piece_of = (lane % BASE) // OVER
+    over_pieces = [jnp.where(piece_of == j, over_t, 0.0) for j in range(PIECES)]
+    place_main = jnp.transpose(main_t).astype(jnp.bfloat16)
+    place_over = jnp.transpose(jnp.concatenate(over_pieces, axis=0)).astype(jnp.bfloat16)
+
+    def split(v):
+        hi = v.astype(jnp.bfloat16)
+        return [hi, (v - hi.astype(jnp.float32)).astype(jnp.bfloat16)]
+
+    def gather(c):
+        block = tokens[:, c * CHUNK : (c + 1) * CHUNK]
+        send[c, :, :CHUNK] = jnp.dot(
+            place_main, block, preferred_element_type=jnp.float32
+        ).astype(jnp.bfloat16)
+        stacked = jnp.concatenate(
+            [block[:, j * LANES : (j + 1) * LANES] for j in range(PIECES)], axis=0
+        )
+        send[c, :, CHUNK:] = jnp.dot(
+            place_over, stacked, preferred_element_type=jnp.float32
+        ).astype(jnp.bfloat16)
+
+    def dispatch(c, p):
+        to = (chip + p) % CHIPS
+        return pltpu.make_async_remote_copy(
+            src_ref=send.at[c, pl.ds(pl.multiple_of(to * BASE, 16), BASE), :],
+            dst_ref=recv.at[c, pl.ds(pl.multiple_of(mine + slot, 16), BASE), :],
+            send_sem=send_sem.at[c, p],
+            recv_sem=recv_sem.at[c, p],
+            device_id={"expert": peer(p)},
+            device_id_type=MESH,
+        )
+
+    def forward(c):
+        return pltpu.make_async_remote_copy(
+            src_ref=recv.at[c, pl.ds(mine, ROWS), :],
+            dst_ref=recv.at[c, pl.ds(mine, ROWS), :],
+            send_sem=fwd_send.at[c],
+            recv_sem=fwd_recv.at[c],
+            device_id={"expert": sibling},
+            device_id_type=MESH,
+        )
+
+    def to_sibling(d):
+        return pltpu.make_async_remote_copy(
+            src_ref=recv.at[d, pl.ds(other, HALF), pl.ds(0, CHUNK)],
+            dst_ref=sib.at[d],
+            send_sem=sib_send.at[d],
+            recv_sem=sib_recv.at[d],
+            device_id={"expert": sibling},
+            device_id_type=MESH,
+        )
+
+    def give_back(d, p):
+        to = (chip + p) % CHIPS
+        return pltpu.make_async_remote_copy(
+            src_ref=send.at[d, pl.ds(pl.multiple_of(to * BASE, 16), BASE), :],
+            dst_ref=back.at[d, pl.ds(slot, BASE), :],
+            send_sem=back_send.at[d, p],
+            recv_sem=back_recv.at[d, p],
+            device_id={"expert": peer(p)},
+            device_id_type=MESH,
+        )
+
+    gather(0)
+    pl.semaphore_wait(barrier, CHIPS)
+    for c in range(chunks):
+        if c > 0:
+            gather(c)
+        for p in range(1, CHIPS):
+            dispatch(c, p).start()
+        recv[c, pl.ds(pl.multiple_of(mine + slot, 16), BASE), :] = send[c, pl.ds(slot, BASE), :]
+
+    n_over = CHIPS * OVER
+    r = iota((PIECES * n_over, ROWS), 0)
+    q = iota((PIECES * n_over, ROWS), 1)
+    unpack = (
+        q == ((r % n_over) // OVER) * BASE + (r // n_over) * OVER + r % OVER
+    ).astype(jnp.bfloat16)
+    rt = iota((ROWS, PIECES * n_over), 1)
+    qt = iota((ROWS, PIECES * n_over), 0)
+    pack = (
+        qt == ((rt % n_over) // OVER) * BASE + (rt // n_over) * OVER + rt % OVER
+    ).astype(jnp.bfloat16)
+
+    def columns(body):
+        whole = units // TILE
+
+        @pl.loop(0, whole)
+        def _(n):
+            body(pl.ds(pl.multiple_of(n * TILE, TILE), TILE))
+
+        if units % TILE:
+            body(pl.ds(whole * TILE, units % TILE))
+
+    for c in range(chunks):
+        for p in range(1, CHIPS):
+            dispatch(c, p).wait_recv()
+        forward(c).start()
+        weight_copy(c, 0).wait()
+        weight_copy(c, 1).wait()
+        forward(c).wait_recv()
+        for h in range(2):
+            spread = jnp.dot(
+                unpack, recv[c, h * HALF : h * HALF + ROWS, CHUNK:], preferred_element_type=jnp.float32
+            ).astype(jnp.bfloat16)
+            for j in range(PIECES):
+                recv[c, h * HALF + ROWS : (h + 1) * HALF, j * LANES : (j + 1) * LANES] = spread[
+                    j * n_over : (j + 1) * n_over
+                ]
+
+        def body(cols, c=c):
+            x = recv[c, :, :CHUNK]
+            g = jnp.dot(x, wg[c, :, cols], preferred_element_type=jnp.float32)
+            u = jnp.dot(x, wu[c, :, cols], preferred_element_type=jnp.float32)
+            if c > 0:
+                g = g + acc_g[:, cols]
+                u = u + acc_u[:, cols]
+            if c < chunks - 1:
+                acc_g[:, cols] = g
+                acc_u[:, cols] = u
+            else:
+                g = g * gate_scale[:, cols]
+                u = u * up_scale[:, cols]
+                hidden[:, cols] = (g / (1.0 + jnp.exp(-g)) * u).astype(jnp.bfloat16)
+
+        columns(body)
+
+    for c in range(chunks):
+        forward(c).wait_send()
+        for p in range(1, CHIPS):
+            dispatch(c, p).wait_send()
+
+    def multiply_down(d):
+        down_copy(d).wait()
+        for t in range(CHUNK // TILE):
+            piece = jnp.dot(
+                hidden[...], wd[d % 2, :, t * TILE : (t + 1) * TILE], preferred_element_type=jnp.float32
+            )
+            lo = d * CHUNK + t * TILE
+            piece = piece * down_scale[pl.ds(chip, 1), lo : lo + TILE]
+            recv[d, :, t * TILE : (t + 1) * TILE] = piece.astype(jnp.bfloat16)
+        to_sibling(d).start()
+        if d + 2 < chunks:
+            down_copy(d + 2).start()
+
+    def finish(d):
+        to_sibling(d).wait_recv()
+        both = recv[d, pl.ds(mine, HALF), :CHUNK].astype(jnp.float32) + sib[d].astype(jnp.float32)
+        both = both.astype(jnp.bfloat16)
+        send[d, :, :CHUNK] = both[:ROWS]
+        stacked = jnp.concatenate(
+            [both[ROWS:, j * LANES : (j + 1) * LANES] for j in range(PIECES)], axis=0
+        )
+        send[d, :, CHUNK:] = jnp.dot(pack, stacked, preferred_element_type=jnp.float32).astype(
+            jnp.bfloat16
+        )
+        for p in range(1, CHIPS):
+            give_back(d, p).start()
+        back[d, pl.ds(slot, BASE), :] = send[d, pl.ds(slot, BASE), :]
+
+    for d in range(chunks):
+        multiply_down(d)
+        if d > 0:
+            finish(d - 1)
+    finish(chunks - 1)
+
+    mix_main = jnp.concatenate(split(main_t * weight), axis=0)
+    mix_over = jnp.concatenate(
+        [part for j in range(PIECES) for part in split(over_pieces[j] * weight)], axis=0
+    )
+    for d in range(chunks):
+        for p in range(1, CHIPS):
+            give_back(d, p).wait_recv()
+        main = jnp.dot(mix_main, back[d, :, :CHUNK], preferred_element_type=jnp.float32)
+        main = main[:toks] + main[toks:]
+        over = jnp.dot(mix_over, back[d, :, CHUNK:], preferred_element_type=jnp.float32)
+        for j in range(PIECES):
+            part = over[2 * j * toks : (2 * j + 1) * toks] + over[(2 * j + 1) * toks : (2 * j + 2) * toks]
+            lo = d * CHUNK + j * LANES
+            out[:, lo : lo + LANES] = (main[:, j * LANES : (j + 1) * LANES] + part).astype(jnp.bfloat16)
+
+    for d in range(chunks):
+        to_sibling(d).wait_send()
+        for p in range(1, CHIPS):
+            give_back(d, p).wait_send()
+
+
+def fused_shards(tokens, expert_ids, gate_fixed, gate_q, up_q, down_q, gate_scale, up_scale, down_scale):
+    toks, width = tokens.shape
+    units = gate_q.shape[1]
+    chunks = width // CHUNK
+    bf16, f32 = jnp.bfloat16, jnp.float32
+    vmem = pl.BlockSpec(memory_space=pltpu.VMEM)
+    hbm = pl.BlockSpec(memory_space=pl.ANY)
+    dma = pltpu.SemaphoreType.DMA
+    return pl.pallas_call(
+        fused_kernel,
+        out_shape=jax.ShapeDtypeStruct((toks, width), bf16),
+        in_specs=[vmem, vmem, vmem, hbm, hbm, hbm, vmem, vmem, vmem],
+        out_specs=vmem,
+        scratch_shapes=[
+            pltpu.VMEM((chunks, CHUNK, units), bf16),
+            pltpu.VMEM((chunks, CHUNK, units), bf16),
+            pltpu.VMEM((2, units, CHUNK), bf16),
+            pltpu.VMEM((chunks, 2 * HALF, WIDE), bf16),
+            pltpu.VMEM((chunks, ROWS, WIDE), bf16),
+            pltpu.VMEM((chunks, ROWS, WIDE), bf16),
+            pltpu.VMEM((2 * HALF, units), f32),
+            pltpu.VMEM((2 * HALF, units), f32),
+            pltpu.VMEM((2 * HALF, units), bf16),
+            pltpu.VMEM((chunks, HALF, CHUNK), bf16),
+            dma((chunks, 2)),
+            dma((2,)),
+            dma((chunks, CHIPS)),
+            dma((chunks, CHIPS)),
+            dma((chunks,)),
+            dma((chunks,)),
+            dma((chunks,)),
+            dma((chunks,)),
+            dma((chunks, CHIPS)),
+            dma((chunks, CHIPS)),
+        ],
+        compiler_params=pltpu.CompilerParams(
+            collective_id=0, has_side_effects=True, vmem_limit_bytes=63 * 1024 * 1024
+        ),
+        cost_estimate=pl.CostEstimate(
+            flops=12 * HALF * width * units, bytes_accessed=6 * width * units, transcendentals=2 * HALF * units
+        ),
+    )(
+        tokens, expert_ids, gate_fixed, gate_q, up_q, down_q,
+        gate_scale.reshape(1, units), up_scale.reshape(1, units), down_scale,
+    )
+
+
 def solution(mesh):
     placed = (
         P(("group", "expert"), None),
@@ -68,6 +377,7 @@
         P("expert"),
         P(),
     )
+    body = fused_shards if mesh.shape["expert"] == 2 * WINDOW else shards
     return jax.shard_map(
-        shards, mesh=mesh, in_specs=placed, out_specs=P(("group", "expert"), None), check_vma=False
-    )
+        body, mesh=mesh, in_specs=placed, out_specs=P(("group", "expert"), None), check_vma=False
+    )

time: 165 us -> 69.5 us (0.42)
  the two profiles are of different devices: /device:TPU:11 before, /device:TPU:0 now
where the time goes in v1:
time: 69.5 us; the launch traced here: 69.1 us
  Pallas kernels  62 us (89%)
  local copies, waits for them, and re-layouts  7.14 us (10%)
    pallas_call x1, Pallas kernels, fused_shards(): pl.pallas_call(fused_kernel, out_shape=jax.ShapeDtypeStruct((toks, width)...  62 us
    unnamed x3, local copies, waits for them, and re-layouts  4.52 us

profile of v1, /device:TPU:0, one launch (start us, length us, event | category | flops | bytes accessed | tf_op | source)
XLA Modules:
  0.0 69.1 jit_solution(3491621244920404284)
XLA Ops:
  0.0 1.3 %reshape.6.gate_scale = f32[1,2688]{1,0:T(1,128)} reshape(f32[2688]{0:T(1024)} %param.15) | data formatting | bytes 21504 | tf_op jit(solution)/shard_map/reshape | solution.py:364
  1.3 1.3 %reshape.7.up_scale = f32[1,2688]{1,0:T(1,128)} reshape(f32[2688]{0:T(1024)} %param.16) | data formatting | bytes 21504 | tf_op jit(solution)/shard_map/reshape | solution.py:364
  2.6 1.4 %copy.10.ids = s32[64,4]{1,0:T(8,128)} copy(s32[64,4]{0,1:T(4,128)} %param.10) | data formatting | bytes 2048 | tf_op args[1]
  4.0 1.4 %copy.11.fixed = s32[64,4]{1,0:T(8,128)} copy(s32[64,4]{0,1:T(4,128)} %param.11) | data formatting | bytes 2048 | tf_op args[2]
  5.4 62.0 %shard_map.91 = bf16[64,3072]{1,0:T(8,128)(2,1)} custom-call(bf16[64,3072]{1,0:T(8,128)(2,1)} %tokens.1, s32[64,4]{1,0:T(8,128)} %copy.10.ids, s32[64,4]{1,0:T(8,128)} %copy.11.fixed, bf16[3072,2688]{1,0:T(8,128)(2,1)} %gate_w.1, bf16[3072,2688]{1,0:T(8,128)(2,1)} %up_w.1, bf16[2688,3072]{1,0:T(8,128)(2,1)} %down_w.1, f32[1,2688]{1,0:T(1,128)} %reshape.6.gate_scale, ...), custom_call_target="tpu_custom_call" | custom-call | flops 14269022208 | bytes 49545216 | tf_op jit(solution)/shard_map/pallas_call | solution.py:329
  67.4 1.8 %copy.13 = bf16[64,3072]{1,0:T(8,128)(2,1)} copy(bf16[64,3072]{1,0:T(8,128)(2,1)} %shard_map.91) | data formatting | bytes 786432

commit v2 on v1

--- a/solution.py
+++ b/solution.py
@@ -79,7 +79,7 @@
 
 def fused_kernel(
     tokens, ids, fixed, gate_w, up_w, down_w, gate_scale, up_scale, down_scale, out,
-    wg, wu, wd, recv, send, back, acc_g, acc_u, hidden, sib,
+    wg, wu, wd, recv, send, back, acc_g, acc_u, hidden, sib, row_g, row_u,
     w_sem, d_sem, send_sem, recv_sem, fwd_send, fwd_recv, sib_send, sib_recv, back_send, back_recv,
 ):
     me = lax.axis_index("expert")
@@ -117,14 +117,18 @@
     for d in range(2):
         down_copy(d).start()
 
+    row_g[...] = gate_scale[...].reshape(1, units)
+    row_u[...] = up_scale[...].reshape(1, units)
+
     lane = iota((toks, LANES), 1)
     chosen = jnp.zeros((toks, LANES), jnp.float32)
     weight = jnp.zeros((toks, LANES), jnp.float32)
-    fx = fixed[...].astype(jnp.float32)
+    fx = jnp.transpose(fixed[...].astype(jnp.float32))
     total = jnp.sum(fx, axis=1, keepdims=True)
-    idv = ids[...]
+    idv = jnp.transpose(ids[...].astype(jnp.float32))
+    owner = (lane // BASE).astype(jnp.float32)
     for k in range(idv.shape[1]):
-        hit = (idv[:, k : k + 1] == lane // BASE).astype(jnp.float32)
+        hit = (idv[:, k : k + 1] == owner).astype(jnp.float32)
         chosen = chosen + hit
         weight = weight + hit * (fx[:, k : k + 1] / total)
     before = (iota((toks, toks), 0) > iota((toks, toks), 1)).astype(jnp.bfloat16)
@@ -252,8 +256,8 @@
                 acc_g[:, cols] = g
                 acc_u[:, cols] = u
             else:
-                g = g * gate_scale[:, cols]
-                u = u * up_scale[:, cols]
+                g = g * row_g[:, cols]
+                u = u * row_u[:, cols]
                 hidden[:, cols] = (g / (1.0 + jnp.exp(-g)) * u).astype(jnp.bfloat16)
 
         columns(body)
@@ -342,6 +346,8 @@
             pltpu.VMEM((2 * HALF, units), f32),
             pltpu.VMEM((2 * HALF, units), bf16),
             pltpu.VMEM((chunks, HALF, CHUNK), bf16),
+            pltpu.VMEM((1, units), f32),
+            pltpu.VMEM((1, units), f32),
             dma((chunks, 2)),
             dma((2,)),
             dma((chunks, CHIPS)),
@@ -360,8 +366,7 @@
             flops=12 * HALF * width * units, bytes_accessed=6 * width * units, transcendentals=2 * HALF * units
         ),
     )(
-        tokens, expert_ids, gate_fixed, gate_q, up_q, down_q,
-        gate_scale.reshape(1, units), up_scale.reshape(1, units), down_scale,
+        tokens, expert_ids.T, gate_fixed.T, gate_q, up_q, down_q, gate_scale, up_scale, down_scale
     )
 
 

time: 69.5 us -> 64 us (0.921)
  local copies, waits for them, and re-layouts: 7.14 us -> 1.77 us
    unnamed x3 -> x1, local copies, waits for them, and re-layouts: 4.52 us -> 1.77 us
    reshape x2 -> x0, local copies, waits for them, and re-layouts: 2.62 us -> none  [the longest x1 1.32 us: fused_shards(): gate_scale.reshape(1, units)]
where the time goes in v2:
time: 64 us; the launch traced here: 63.8 us
  Pallas kernels  62 us (97%)
  local copies, waits for them, and re-layouts  1.77 us (3%)
    pallas_call x1, Pallas kernels, fused_shards(): pl.pallas_call(fused_kernel, out_shape=jax.ShapeDtypeStruct((toks, width)...  62 us
    unnamed x1, local copies, waits for them, and re-layouts  1.77 us

profile of v2, /device:TPU:0, one launch (start us, length us, event | category | flops | bytes accessed | tf_op | source)
XLA Modules:
  0.0 63.8 jit_solution(18278482255194700662)
XLA Ops:
  0.0 62.0 %shard_map.91 = bf16[64,3072]{1,0:T(8,128)(2,1)} custom-call(bf16[64,3072]{1,0:T(8,128)(2,1)} %tokens.1, s32[4,64]{1,0:T(4,128)} %bitcast.2, s32[4,64]{1,0:T(4,128)} %bitcast.3, bf16[3072,2688]{1,0:T(8,128)(2,1)} %gate_w.1, bf16[3072,2688]{1,0:T(8,128)(2,1)} %up_w.1, bf16[2688,3072]{1,0:T(8,128)(2,1)} %down_w.1, f32[2688]{0:T(1024)} %gate_scale.1, ...), custom_call_target="tpu_custom_call" | custom-call | flops 14269022208 | bytes 49545216 | tf_op jit(solution)/shard_map/pallas_call | solution.py:333
  62.0 1.8 %copy.11 = bf16[64,3072]{1,0:T(8,128)(2,1)} copy(bf16[64,3072]{1,0:T(8,128)(2,1)} %shard_map.91) | data formatting | bytes 786432

commit v3 on v2

--- a/solution.py
+++ b/solution.py
@@ -276,6 +276,8 @@
             lo = d * CHUNK + t * TILE
             piece = piece * down_scale[pl.ds(chip, 1), lo : lo + TILE]
             recv[d, :, t * TILE : (t + 1) * TILE] = piece.astype(jnp.bfloat16)
+            if t == 0 and d > 0:
+                finish(d - 1)
         to_sibling(d).start()
         if d + 2 < chunks:
             down_copy(d + 2).start()
@@ -297,8 +299,6 @@
 
     for d in range(chunks):
         multiply_down(d)
-        if d > 0:
-            finish(d - 1)
     finish(chunks - 1)
 
     mix_main = jnp.concatenate(split(main_t * weight), axis=0)

time: 64 us -> 63.2 us (0.988)
  Pallas kernels: 62 us -> 61.2 us
    pallas_call x1, Pallas kernels: 62 us -> 61.2 us  [fused_shards(): pl.pallas_call(fused_kernel, out_shape=jax.ShapeDtypeStruct((toks, width)...]
where the time goes in v3:
time: 63.2 us; the launch traced here: 63 us
  Pallas kernels  61.2 us (97%)
  local copies, waits for them, and re-layouts  1.77 us (3%)
    pallas_call x1, Pallas kernels, fused_shards(): pl.pallas_call(fused_kernel, out_shape=jax.ShapeDtypeStruct((toks, width)...  61.2 us
    unnamed x1, local copies, waits for them, and re-layouts  1.77 us

profile of v3, /device:TPU:0, one launch (start us, length us, event | category | flops | bytes accessed | tf_op | source)
XLA Modules:
  0.0 63.0 jit_solution(526374089113959297)
XLA Ops:
  0.0 61.2 %shard_map.91 = bf16[64,3072]{1,0:T(8,128)(2,1)} custom-call(bf16[64,3072]{1,0:T(8,128)(2,1)} %tokens.1, s32[4,64]{1,0:T(4,128)} %bitcast.2, s32[4,64]{1,0:T(4,128)} %bitcast.3, bf16[3072,2688]{1,0:T(8,128)(2,1)} %gate_w.1, bf16[3072,2688]{1,0:T(8,128)(2,1)} %up_w.1, bf16[2688,3072]{1,0:T(8,128)(2,1)} %down_w.1, f32[2688]{0:T(1024)} %gate_scale.1, ...), custom_call_target="tpu_custom_call" | custom-call | flops 14269022208 | bytes 49545216 | tf_op jit(solution)/shard_map/pallas_call | solution.py:333
  61.2 1.8 %copy.11 = bf16[64,3072]{1,0:T(8,128)(2,1)} copy(bf16[64,3072]{1,0:T(8,128)(2,1)} %shard_map.91) | data formatting | bytes 786432
